TPU v7x, 128 devices: a whole 4x4x4 slice. The times are simulated.
128 devices in a mesh: dp: 16 (over z, y), seq: 8 (over x, core).
Axes of the slice: x: 4, y: 4, z: 4, core: 2. Of those that a mesh axis runs over, the one named last changes fastest.
Arguments:
- acts: bfloat16 [32, 512, 4608], P('dp', 'seq'), may hold values from -20 to 20, as said below
- grads: bfloat16 [32, 512, 18432], P('dp', 'seq'), may hold values from -0.00045670236 to 0.00045670236, as said below
Outputs:
- update: bfloat16 [4608, 18432], P('dp', 'seq')
- norms: float32 [32], P('dp')
Inputs may be any that keep to these rules, and one draw needn't show every extreme that they name: `acts`: entries of order one. `grads`: independent entries, small: magnitudes under 2000 / (21 * sqrt(43486543872)).
All inputs are finite; a program needn't handle non-finite values.
Results may differ from a plain program's by a relative error of at most 0.025.
Values may be sent and summed in bfloat16 or wider, within the bound.
No kernel may reach another device: no remote copies, remote signals or barrier semaphores. Data moves between devices by JAX's collectives and lax.ppermute only.
A program may use at most 128 MiB of HBM per device.

v0:
```python
import math

import jax
import jax.numpy as jnp
from jax import lax
from jax.sharding import PartitionSpec as P


def on_device(acts, grads):
    seq_count = lax.axis_size("seq")
    replica_count = lax.axis_size("dp")
    examples, local_len, width = acts.shape
    hidden = grads.shape[2]
    complete_matrix = lax.all_gather(acts, "seq", axis=1, tiled=True)
    column_total = lax.all_to_all(grads, "seq", split_axis=2, concat_axis=1, tiled=True)
    gradient_gram_matrix = jnp.einsum(
        "slf,smf->slm", column_total, column_total, preferred_element_type=jnp.float32
    )
    activation_gram_matrix = jnp.einsum(
        "nih,nfh->nif", complete_matrix, complete_matrix, preferred_element_type=jnp.float32
    )
    partial_value = jnp.sum(activation_gram_matrix * gradient_gram_matrix, axis=(1, 2))
    squared = lax.psum(partial_value, "seq")
    norms = jnp.sqrt(squared)
    clip = jnp.minimum(1.0, 1.0 / (norms + 1e-06))
    factor = math.sqrt(width * hidden / (examples * replica_count))
    scaled = (column_total * (clip * factor)[:, None, None]).astype(jnp.bfloat16)
    flat_acts = complete_matrix.reshape(-1, width)
    flat_scaled = scaled.reshape(-1, hidden // seq_count)
    total = lax.psum_scatter(
        lax.dot_general(
            flat_acts, flat_scaled, (((0,), (0,)), ((), ())), preferred_element_type=jnp.float32
        ).astype(jnp.bfloat16),
        "dp",
        scatter_dimension=0,
        tiled=True,
    )
    return (total, norms)


def solution(mesh):
    return jax.shard_map(
        on_device,
        mesh=mesh,
        in_specs=(P("dp", "seq", None), P("dp", "seq", None)),
        out_specs=(P("dp", "seq"), P("dp")),
        check_vma=False,
    )
```

profile of v0, /device:TPU:4, one launch (start us, length us, event | category | flops | bytes accessed | tf_op | source)
XLA Modules:
  0.0 369.9 jit_solution(17695459624670924494)
XLA Ops:
  7.2 0.0 all-gather.2.cloned.1.call-start
  7.2 0.7 all-gather.2.cloned.1.call-update
  7.9 0.0 reduce-scatter.4.cloned.1.call-start
  7.9 19.9 %copy.7 = bf16[2,64,18432]{1,0,2:T(2,128)(2,1)} copy(bf16[2,64,18432]{2,1,0:T(8,128)(2,1)} %param.3) | data formatting | bytes 9437184 | tf_op args[1]
  27.9 11.4 %reshape.10 = bf16[8,2,147456]{2,1,0:T(2,128)(2,1)} reshape(bf16[18432,2,64]{2,1,0:T(2,128)(2,1)} %bitcast.19) | data formatting | bytes 9437184
  39.3 74.4 %all_to_all.18 = bf16[8,2,147456]{2,1,0:T(2,128)(2,1)} all-to-all(bf16[8,2,147456]{2,1,0:T(2,128)(2,1)} %reshape.10), channel_id=1, replica_groups=mesh['dp'=16,'seq'=8] {'seq'}, dimensions={0} | all-to-all | bytes 9437184 | tf_op jit(solution)/shard_map/all_to_all | solution.py:15
  113.7 11.2 %reshape.11 = bf16[18432,2,64]{2,1,0:T(2,128)(2,1)} reshape(bf16[8,2,147456]{2,1,0:T(2,128)(2,1)} %all_to_all.18) | data formatting | bytes 9437184
  124.9 21.1 %copy.8 = bf16[2,64,8,2304]{3,1,2,0:T(8,128)(2,1)} copy(bf16[2,64,8,2304]{1,0,3,2:T(2,128)(2,1)} %bitcast.18) | data formatting | bytes 9437184 | tf_op jit(solution)/shard_map/all_to_all | solution.py:15
  146.0 0.0 all-gather.2.cloned.1.call-done
  146.0 0.0 copy-start
  146.0 10.5 %fusion.2 = f32[2,512,512]{2,1,0:T(8,128)S(1)} fusion(bf16[2,512,4608]{2,1,0:T(8,128)(2,1)} %all-gather.2.cloned.1.call-done), kind=kOutput, calls=%fused_computation.6 | convolution fusion | flops 4831838208 | bytes 11534336 | tf_op jit(solution)/shard_map/nih,nfh->nif/dot_general | solution.py:19
  156.6 0.0 copy-done
  156.6 2.9 multiply_reduce_fusion
  159.5 12.2 %psum.7 = f32[2]{0:T(128)S(1)} all-reduce(f32[2]{0:T(128)S(1)} %multiply_reduce_fusion), channel_id=1, replica_groups=mesh['dp'=16,'seq'=8] {'seq'}, use_global_device_ids=true, to_apply=%region_1.0 | all-reduce | flops 2 | bytes 16 | tf_op jit(solution)/shard_map/psum | solution.py:23
  171.7 0.5 minimum_multiply_fusion
  172.2 29.3 %fusion = bf16[4608,2304]{0,1:T(8,128)(2,1)} fusion(bf16[2,512,4608]{2,1,0:T(8,128)(2,1)} %all-gather.2.cloned.1.call-done, bf16[2,512,2304]{2,1,0:T(8,128)(2,1)} %bitcast.20, f32[2]{0:T(128)S(1)} %get-tuple-element.6), kind=kOutput, calls=%fused_computation.1 | convolution fusion | flops 21760966656 | bytes 35389448 | tf_op jit(solution)/shard_map/dot_general | solution.py:31
  201.5 25.5 %copy.12 = bf16[4608,2304]{1,0:T(8,128)(2,1)} copy(bf16[4608,2304]{0,1:T(8,128)(2,1)} %fusion) | data formatting | bytes 42467328
  227.0 0.0 reduce-scatter.4.cloned.1.call-update
  227.1 136.0 %reduce-scatter.4.cloned.1.call-done = bf16[288,2304]{1,0:T(8,128)(2,1)} async-done(((bf16[4608,2304]{1,0:T(8,128)(2,1)}), bf16[288,2304]{1,0:T(8,128)(2,1)}) %reduce-scatter.4.cloned.1.call-update) | async-done | bytes 1327120
Async XLA Ops:
  7.2 138.9 %all-gather.2.cloned.1.call-start = ((), (), s32[]{:S(2)}) async-start(), calls=%async_computation.2 | async-start | bytes 10616832 | tf_op jit(solution)/shard_map/all_gather | solution.py:14
  7.9 355.1 %reduce-scatter.4.cloned.1.call-start = ((), (), s32[]{:S(2)}) async-start(), calls=%async_computation.3 | async-start | bytes 22560768
  146.0 10.5 %copy-start = (bf16[2,64,8,2304]{3,1,2,0:T(8,128)(2,1)S(1)}, bf16[2,64,8,2304]{3,1,2,0:T(8,128)(2,1)}, u32[]{:S(2)}) copy-start(bf16[2,64,8,2304]{3,1,2,0:T(8,128)(2,1)} %copy.8) | copy-start | bytes 14155780
Sparse Core Ops, SparseCore 0:
  9.7 86.6 all-gather.1
  227.2 135.8 reduce-scatter.3
where the time goes:
time: 373 us; the launch traced here: 370 us
  waiting for transfers between devices  137 us (37%)
  local copies, waits for them, and re-layouts  89.2 us (24%)
  blocking collectives  86.6 us (23%)
  matrix products  42.7 us (11%)
  between operations  14.1 us (4%)
    unnamed x3, waiting for transfers between devices  137 us
    all_to_all x1, blocking collectives, on_device(): lax.all_to_all(grads, 'seq', split_axis=2, concat_axis=1, tiled=True)  74.4 us
    unnamed x6, local copies, waits for them, and re-layouts  68.1 us
    dot_general x1, matrix products, on_device(): lax.dot_general(flat_acts, flat_scaled, (((0,), (0,)), ((), ())), preferr...  29.3 us
    all_to_all x1, local copies, waits for them, and re-layouts, on_device(): lax.all_to_all(grads, 'seq', split_axis=2, concat_axis=1, tiled=True)  21.1 us
    psum x1, blocking collectives, on_device(): squared = lax.psum(partial_value, 'seq')  12.2 us
    dot_general x1, matrix products, on_device(): jnp.einsum('nih,nfh->nif', complete_matrix, complete_matrix, preferred_el...  10.5 us
  transfers between devices with their start and end apart: 2, of which 1 were waited for; matrix products, arithmetic and copies ran while one was open for 17% of the time, Pallas kernels for 0%

commit v1 on v0

v1 whole, which is shorter than its diff:
```python
import functools
import math

import jax
import jax.numpy as jnp
from jax import lax
from jax.experimental import pallas as pl
from jax.experimental.pallas import tpu as pltpu
from jax.sharding import PartitionSpec as P

ORDERS = ((4, 12, 1, 3), (12, 4, 3, 1), (1, 3, 4, 12), (3, 1, 12, 4))
WIDTHS = (640, 640, 512, 512)


def block_order(masks):
    order = [0]
    for mask in reversed(masks):
        order = order + [mask ^ k for k in order]
    return order


def exchange(value, axis, mask):
    return lax.ppermute(value, axis, [(i, i ^ mask) for i in range(lax.axis_size(axis))])


def product_kernel(index_ref, *refs):
    *a_refs, g_ref, out_ref = refs
    rows = jnp.concatenate([a[0] for a in a_refs], axis=0)
    out_ref[...] = jnp.dot(rows, g_ref[...], preferred_element_type=jnp.float32).astype(out_ref.dtype)


def product(a_blocks, g, index, group):
    count = index.shape[0]
    _, block, tokens = a_blocks.shape
    width = g.shape[1]
    a_specs = [
        pl.BlockSpec((1, block, tokens), functools.partial(lambda j, i, index_ref: (index_ref[i * group + j], 0, 0), j))
        for j in range(group)
    ]
    return pl.pallas_call(
        product_kernel,
        grid_spec=pltpu.PrefetchScalarGridSpec(
            num_scalar_prefetch=1,
            grid=(count // group,),
            in_specs=[*a_specs, pl.BlockSpec((tokens, width), lambda i, index_ref: (0, 0))],
            out_specs=pl.BlockSpec((group * block, width), lambda i, index_ref: (i, 0)),
        ),
        out_shape=jax.ShapeDtypeStruct((count * block, width), jnp.bfloat16),
        compiler_params=pltpu.CompilerParams(vmem_limit_bytes=40 * 1024 * 1024),
        cost_estimate=pl.CostEstimate(
            flops=2 * count * block * tokens * width,
            bytes_accessed=2 * (count * block * tokens + tokens * width + count * block * width),
            transcendentals=0,
        ),
    )(index, *([a_blocks] * group), g)


def turn_kernel(in_ref, out_ref):
    out_ref[...] = in_ref[...].T


def turn(value):
    tokens, width = value.shape
    step = 4
    return pl.pallas_call(
        turn_kernel,
        grid=(step,),
        in_specs=[pl.BlockSpec((tokens, width // step), lambda i: (0, i))],
        out_specs=pl.BlockSpec((width // step, tokens), lambda i: (i, 0)),
        out_shape=jax.ShapeDtypeStruct((width, tokens), value.dtype),
    )(value)


def join_kernel(in_ref, out_ref):
    for s in range(in_ref.shape[0]):
        out_ref[:, s * in_ref.shape[2] : (s + 1) * in_ref.shape[2]] = in_ref[s]


def join(value):
    n, rows, lanes = value.shape
    step = 8
    return pl.pallas_call(
        join_kernel,
        grid=(step,),
        in_specs=[pl.BlockSpec((n, rows // step, lanes), lambda i: (0, i, 0))],
        out_specs=pl.BlockSpec((rows // step, n * lanes), lambda i: (i, 0)),
        out_shape=jax.ShapeDtypeStruct((rows, n * lanes), value.dtype),
    )(value)


def split_kernel(in_ref, *out_refs):
    low = 0
    for out_ref in out_refs:
        size = out_ref.shape[2]
        out_ref[0] = in_ref[:, low : low + size]
        low += size


def split(value, n, widths):
    rows, total = value.shape
    return pl.pallas_call(
        split_kernel,
        grid=(n,),
        in_specs=[pl.BlockSpec((rows, total // n), lambda i: (0, i))],
        out_specs=[pl.BlockSpec((1, rows, w), lambda i: (i, 0, 0)) for w in widths],
        out_shape=[jax.ShapeDtypeStruct((n, rows, w), value.dtype) for w in widths],
    )(value)


def add(a, b):
    return (a.astype(jnp.float32) + b.astype(jnp.float32)).astype(jnp.bfloat16)


def on_device(acts, grads):
    seq_count = lax.axis_size("seq")
    replica_count = lax.axis_size("dp")
    examples, local_len, width = acts.shape
    hidden = grads.shape[2]
    local = examples * local_len
    tokens = seq_count * local
    block = width // replica_count
    me = lax.axis_index("dp")

    a_t = join(lax.all_gather(turn(acts.reshape(local, width)), "seq", axis=0))
    example = (jnp.arange(tokens) // local_len) % examples
    same = example[:, None] == example[None, :]
    act_gram = lax.dot_general(a_t, a_t, (((0,), (0,)), ((), ())), preferred_element_type=jnp.float32)
    act_gram = jnp.where(same, act_gram, 0.0)

    parts = []
    rows_sum = jnp.zeros((tokens,), jnp.float32)
    for piece in split(grads.reshape(local, hidden), seq_count, WIDTHS):
        piece = lax.all_to_all(piece, "seq", split_axis=0, concat_axis=0, tiled=True)
        piece = piece.reshape(tokens, -1)
        gram = lax.dot_general(piece, piece, (((1,), (1,)), ((), ())), preferred_element_type=jnp.float32)
        rows_sum = rows_sum + jnp.sum(act_gram * gram, axis=1)
        parts.append(piece)
    partial_value = jnp.sum(rows_sum.reshape(seq_count, examples, local_len), axis=(0, 2))
    norms = jnp.sqrt(lax.psum(partial_value, "seq"))
    clip = jnp.minimum(1.0, 1.0 / (norms + 1e-06))
    factor = math.sqrt(width * hidden / (examples * replica_count))
    scale = jnp.tile(jnp.repeat(clip * factor, local_len), seq_count)[:, None]

    a_blocks = a_t.reshape(replica_count, block, tokens)
    outs = []
    for masks, piece in zip(ORDERS, parts):
        scaled = (piece * scale).astype(jnp.bfloat16)
        order = me ^ jnp.array(block_order(masks), jnp.int32)
        half = replica_count // 2
        send = product(a_blocks, scaled, order[half:], 4)
        keep = product(a_blocks, scaled, order[:half], 4)
        received = exchange(send, "dp", masks[0])
        for mask in masks[1:]:
            rows = keep.shape[0] // 2
            send = add(keep[rows:], received[rows:])
            sent = exchange(send, "dp", mask)
            keep = add(keep[:rows], received[:rows])
            received = sent
        outs.append(add(keep, received))
    return (jnp.concatenate(outs, axis=1), norms)


def solution(mesh):
    return jax.shard_map(
        on_device,
        mesh=mesh,
        in_specs=(P("dp", "seq", None), P("dp", "seq", None)),
        out_specs=(P("dp", "seq"), P("dp")),
        check_vma=False,
    )
```

time: 373 us -> 347 us (0.930)
  local copies, waits for them, and re-layouts: 89.2 us -> 4.22 us
  Pallas kernels: 0 us -> 57.1 us
  blocking collectives: 86.6 us -> 39.8 us
  starting transfers between devices: 0.08 us -> 33.8 us
  other arithmetic: 0.52 us -> 16.2 us
  matrix products: 42.7 us -> 30.4 us
  waiting for transfers between devices: 137 us -> 146 us
    unnamed x3 -> x1, waiting for transfers between devices: 137 us -> 0.02 us
    ppermute x0 -> x16, waiting for transfers between devices: none -> 103 us  [exchange(): lax.ppermute(value, axis, [(i, i ^ mask) for i in range(lax.axis_size(axi...]
    unnamed x6 -> x12, local copies, waits for them, and re-layouts: 68.1 us -> 3.69 us
    pallas_call x0 -> x11, Pallas kernels: none -> 57.1 us  [the longest x8 36.1 us: product(): pl.pallas_call(product_kernel, grid_spec=pltpu.PrefetchScalarGridSpec(num...]
    all_to_all x1, blocking collectives: 74.4 us -> 28.2 us  [on_device(): lax.all_to_all(piece, 'seq', split_axis=0, concat_axis=0, tiled=True)]
    all_gather x1, waiting for transfers between devices: 0.01 us -> 34.1 us  [on_device(): a_t = join(lax.all_gather(turn(acts.reshape(local, width)), 'seq', axis=0))]
    all_to_all x1 -> x0, local copies, waits for them, and re-layouts: 21.1 us -> none  [on_device(): lax.all_to_all(grads, 'seq', split_axis=2, concat_axis=1, tiled=True)]
    all_to_all x0 -> x3, starting transfers between devices: none -> 17.4 us  [on_device(): lax.all_to_all(piece, 'seq', split_axis=0, concat_axis=0, tiled=True)]
  transfers between devices with their start and end apart: 2 -> 20, of which waited for: 1 -> 12; matrix products, arithmetic and copies ran while one was open for 17% -> 12% of each run, Pallas kernels for 0% -> 14%
where the time goes in v1:
time: 347 us; the launch traced here: 342 us
  waiting for transfers between devices  146 us (42%)
  Pallas kernels  57.1 us (16%)
  blocking collectives  39.8 us (11%)
  starting transfers between devices  33.8 us (10%)
  matrix products  30.4 us (9%)
  other arithmetic  16.2 us (5%)
  between operations  14.3 us (4%)
  local copies, waits for them, and re-layouts  4.22 us (1%)
    ppermute x16, waiting for transfers between devices, exchange(): lax.ppermute(value, axis, [(i, i ^ mask) for i in range(lax.axis_size(axi...  103 us
    pallas_call x8, Pallas kernels, product(): pl.pallas_call(product_kernel, grid_spec=pltpu.PrefetchScalarGridSpec(num...  36.1 us
    all_gather x1, waiting for transfers between devices, on_device(): a_t = join(lax.all_gather(turn(acts.reshape(local, width)), 'seq', axis=0))  34.1 us
    all_to_all x1, blocking collectives, on_device(): lax.all_to_all(piece, 'seq', split_axis=0, concat_axis=0, tiled=True)  28.2 us
    dot_general x1, matrix products, on_device(): lax.dot_general(a_t, a_t, (((0,), (0,)), ((), ())), preferred_element_typ...  18.6 us
    all_to_all x3, starting transfers between devices, on_device(): lax.all_to_all(piece, 'seq', split_axis=0, concat_axis=0, tiled=True)  17.4 us
    ppermute x16, starting transfers between devices, exchange(): lax.ppermute(value, axis, [(i, i ^ mask) for i in range(lax.axis_size(axi...  16.3 us
    convert_element_type x16, other arithmetic, add(): return (a.astype(jnp.float32) + b.astype(jnp.float32)).astype(jnp.bfloat16)  12 us
  transfers between devices with their start and end apart: 20, of which 12 were waited for; matrix products, arithmetic and copies ran while one was open for 12% of the time, Pallas kernels for 14%

profile of v1, /device:TPU:4, one launch (start us, length us, event | category | flops | bytes accessed | tf_op | source)
XLA Modules:
  0.0 341.5 jit_solution(2341286236832434500)
XLA Ops:
  7.2 3.7 %shard_map.77 = bf16[4608,128]{1,0:T(8,128)(2,1)} custom-call(bf16[128,4608]{1,0:T(8,128)(2,1)} %bitcast.61), custom_call_target="tpu_custom_call" | custom-call | tf_op jit(solution)/shard_map/pallas_call | solution.py:65
  10.9 6.9 %shard_map.79 = (bf16[8,128,640]{2,1,0:T(8,128)(2,1)}, bf16[8,128,640]{2,1,0:T(8,128)(2,1)}, bf16[8,128,512]{2,1,0:T(8,128)(2,1)}, bf16[8,128,512]{2,1,0:T(8,128)(2,1)}) custom-call(bf16[128,18432]{1,0:T(8,128)(2,1)} %bitcast.58), custom_call_target="tpu_custom_call" | custom-call | tf_op jit(solution)/shard_map/pallas_call | solution.py:101
  17.8 28.2 %all_to_all.20 = bf16[8,128,512]{2,1,0:T(8,128)(2,1)S(1)} all-to-all(bf16[8,128,512]{2,1,0:T(8,128)(2,1)} %get-tuple-element.9), channel_id=1, replica_groups=mesh['dp'=16,'seq'=8] {'seq'}, dimensions={0} | all-to-all | bytes 2097152 | tf_op jit(solution)/shard_map/all_to_all | solution.py:133
  46.0 6.9 %all-to-all-start.2 = ((bf16[8,128,512]{2,1,0:T(8,128)(2,1)}), bf16[8,128,512]{2,1,0:T(8,128)(2,1)S(1)}, u32[]{:S(2)}, u32[]{:S(2)}) async-start(bf16[8,128,512]{2,1,0:T(8,128)(2,1)} %get-tuple-element.8), calls=%async_computation.2 | async-start | bytes 2097152 | tf_op jit(solution)/shard_map/all_to_all | solution.py:133
  53.1 34.1 %all-gather.3.cloned.1.call-done = bf16[36864,128]{1,0:T(8,128)(2,1)} async-done(((bf16[4608,128]{1,0:T(8,128)(2,1)}), bf16[36864,128]{1,0:T(8,128)(2,1)}) %all-gather.3.cloned.1.call-update) | async-done | bytes 9437200 | tf_op jit(solution)/shard_map/all_gather | solution.py:124
  87.2 10.5 %shard_map.78 = bf16[4608,1024]{1,0:T(8,128)(2,1)} custom-call(bf16[8,4608,128]{2,1,0:T(8,128)(2,1)} %bitcast.56), custom_call_target="tpu_custom_call" | custom-call | tf_op jit(solution)/shard_map/pallas_call | solution.py:82
  97.7 5.7 %all-to-all-start = ((bf16[8,128,640]{2,1,0:T(8,128)(2,1)}), bf16[8,128,640]{2,1,0:T(8,128)(2,1)S(1)}, u32[]{:S(2)}, u32[]{:S(2)}) async-start(bf16[8,128,640]{2,1,0:T(8,128)(2,1)} %get-tuple-element.6), calls=%async_computation | async-start | bytes 2621440 | tf_op jit(solution)/shard_map/all_to_all | solution.py:133
  103.4 18.6 %fusion.8 = f32[1024,1024]{0,1:T(8,128)} fusion(bf16[4608,1024]{1,0:T(8,128)(2,1)} %shard_map.78), kind=kOutput, calls=%fused_computation.60 | convolution fusion | flops 9663676416 | bytes 13631488 | tf_op jit(solution)/shard_map/dot_general | solution.py:127
  122.0 4.8 %all-to-all-start.1 = ((bf16[8,128,640]{2,1,0:T(8,128)(2,1)}), bf16[8,128,640]{2,1,0:T(8,128)(2,1)}, u32[]{:S(2)}, u32[]{:S(2)}) async-start(bf16[8,128,640]{2,1,0:T(8,128)(2,1)} %get-tuple-element.7), calls=%async_computation.1 | async-start | bytes 2621440 | tf_op jit(solution)/shard_map/all_to_all | solution.py:133
  126.8 3.7 %multiply_reduce_fusion = f32[1024]{0:T(1024)S(1)} fusion(f32[1024,1024]{0,1:T(8,128)} %fusion.8, bf16[1024,512]{1,0:T(8,128)(2,1)S(1)} %bitcast.59, s32[1024]{0:T(1024)S(1)} %add_select_fusion), kind=kOutput, calls=%fused_computation | convolution fusion | flops 1077935104 | bytes 5251072 | tf_op jit(solution)/shard_map/dot_general | solution.py:135
  133.8 8.8 %all-to-all-done.1 = bf16[8,128,640]{2,1,0:T(8,128)(2,1)} async-done(((bf16[8,128,640]{2,1,0:T(8,128)(2,1)}), bf16[8,128,640]{2,1,0:T(8,128)(2,1)}, u32[]{:S(2)}, u32[]{:S(2)}) %all-to-all-start.1) | async-done | bytes 1310752 | tf_op jit(solution)/shard_map/all_to_all | solution.py:133
  142.5 4.8 %multiply_reduce_fusion.2 = f32[1024]{0:T(1024)S(1)} fusion(f32[1024,1024]{0,1:T(8,128)} %fusion.8, bf16[1024,640]{1,0:T(8,128)(2,1)} %bitcast.5, s32[1024]{0:T(1024)S(1)} %add_select_fusion), kind=kOutput, calls=%fused_computation.2 | convolution fusion | flops 1346370560 | bytes 5513216 | tf_op jit(solution)/shard_map/dot_general | solution.py:135
  147.7 11.7 %psum.7 = f32[2]{0:T(128)S(1)} all-reduce(f32[2]{0:T(128)S(1)} %reduce_sum.49), channel_id=1, replica_groups=mesh['dp'=16,'seq'=8] {'seq'}, use_global_device_ids=true, to_apply=%region_5.6 | all-reduce | flops 2 | bytes 16 | tf_op jit(solution)/shard_map/psum | solution.py:139
  160.5 3.7 %copy-done = bf16[4608,1024]{1,0:T(8,128)(2,1)S(1)} copy-done((bf16[4608,1024]{1,0:T(8,128)(2,1)S(1)}, bf16[4608,1024]{1,0:T(8,128)(2,1)}, u32[]{:S(2)}) %copy-start) | copy-done | bytes 9437208
  164.2 4.4 %shard_map.87 = bf16[2304,512]{1,0:T(8,128)(2,1)} custom-call(s32[8]{0:T(128)S(1)} %get-tuple-element.39.index_ref, bf16[16,288,1024]{2,1,0:T(8,128)(2,1)S(1)} %bitcast.24, bf16[16,288,1024]{2,1,0:T(8,128)(2,1)S(1)} %bitcast.25, bf16[16,288,1024]{2,1,0:T(8,128)(2,1)S(1)} %bitcast.26, bf16[16,288,1024]{2,1,0:T(8,128)(2,1)S(1)} %bitcast.27, ...), custom_call_target="tpu_custom_call" | custom-call | flops 2415919104 | bytes 8126464 | tf_op jit(solution)/shard_map/pallas_call | solution.py:40
  171.5 4.4 %shard_map.85 = bf16[2304,512]{1,0:T(8,128)(2,1)} custom-call(s32[8]{0:T(128)S(1)} %get-tuple-element.37.index_ref, bf16[16,288,1024]{2,1,0:T(8,128)(2,1)S(1)} %bitcast.28, bf16[16,288,1024]{2,1,0:T(8,128)(2,1)S(1)} %bitcast.29, bf16[16,288,1024]{2,1,0:T(8,128)(2,1)S(1)} %bitcast.30, bf16[16,288,1024]{2,1,0:T(8,128)(2,1)S(1)} %bitcast.31, ...), custom_call_target="tpu_custom_call" | custom-call | flops 2415919104 | bytes 8126464 | tf_op jit(solution)/shard_map/pallas_call | solution.py:40
  178.0 5.7 %shard_map.83 = bf16[2304,640]{1,0:T(8,128)(2,1)} custom-call(s32[8]{0:T(128)S(1)} %get-tuple-element.35.index_ref, bf16[16,288,1024]{2,1,0:T(8,128)(2,1)S(1)} %bitcast.32, bf16[16,288,1024]{2,1,0:T(8,128)(2,1)S(1)} %bitcast.33, bf16[16,288,1024]{2,1,0:T(8,128)(2,1)S(1)} %bitcast.34, bf16[16,288,1024]{2,1,0:T(8,128)(2,1)S(1)} %bitcast.35, ...), custom_call_target="tpu_custom_call" | custom-call | flops 3019898880 | bytes 8978432 | tf_op jit(solution)/shard_map/pallas_call | solution.py:40
  183.7 3.8 %collective-permute-start.4 = (bf16[2304,640]{1,0:T(8,128)(2,1)}, bf16[2304,640]{1,0:T(8,128)(2,1)}, u32[]{:S(2)}, u32[]{:S(2)}) collective-permute-start(bf16[2304,640]{1,0:T(8,128)(2,1)} %shard_map.83), channel_id=1, source_target_pairs={{0,96},{8,104},{16,112},{24,120},{32,64},{40,72},{48,80},{56,88},{... | collective-permute-start | bytes 8847368 | tf_op jit(solution)/shard_map/ppermute | solution.py:23
  187.5 5.8 %shard_map.81 = bf16[2304,640]{1,0:T(8,128)(2,1)} custom-call(s32[8]{0:T(128)S(1)} %get-tuple-element.33.index_ref, bf16[16,288,1024]{2,1,0:T(8,128)(2,1)S(1)} %bitcast.39, bf16[16,288,1024]{2,1,0:T(8,128)(2,1)S(1)} %bitcast.37, bf16[16,288,1024]{2,1,0:T(8,128)(2,1)S(1)} %bitcast.38, bf16[16,288,1024]{2,1,0:T(8,128)(2,1)S(1)} %bitcast.36, ...), custom_call_target="tpu_custom_call" | custom-call | flops 3019898880 | bytes 8978432 | tf_op jit(solution)/shard_map/pallas_call | solution.py:40
  193.4 3.4 shard_map.86
  196.7 3.4 shard_map.84
  200.1 4.6 %shard_map.82 = bf16[2304,640]{1,0:T(8,128)(2,1)S(1)} custom-call(s32[8]{0:T(128)S(1)} %get-tuple-element.34.index_ref, bf16[16,288,1024]{2,1,0:T(8,128)(2,1)S(1)} %bitcast.48, bf16[16,288,1024]{2,1,0:T(8,128)(2,1)S(1)} %bitcast.49, bf16[16,288,1024]{2,1,0:T(8,128)(2,1)S(1)} %bitcast.50, bf16[16,288,1024]{2,1,0:T(8,128)(2,1)S(1)} %bitcast.51, ...), custom_call_target="tpu_custom_call" | custom-call | flops 3019898880 | bytes 8978432 | tf_op jit(solution)/shard_map/pallas_call | solution.py:40
  204.7 4.6 %shard_map.80 = bf16[2304,640]{1,0:T(8,128)(2,1)S(1)} custom-call(s32[8]{0:T(128)S(1)} %get-tuple-element.32.index_ref, bf16[16,288,1024]{2,1,0:T(8,128)(2,1)S(1)} %bitcast.52, bf16[16,288,1024]{2,1,0:T(8,128)(2,1)S(1)} %bitcast.53, bf16[16,288,1024]{2,1,0:T(8,128)(2,1)S(1)} %bitcast.54, bf16[16,288,1024]{2,1,0:T(8,128)(2,1)S(1)} %bitcast.55, ...), custom_call_target="tpu_custom_call" | custom-call | flops 3019898880 | bytes 8978432 | tf_op jit(solution)/shard_map/pallas_call | solution.py:40
  209.3 13.3 %collective-permute-done.12 = bf16[2304,512]{1,0:T(8,128)(2,1)} collective-permute-done((bf16[2304,512]{1,0:T(8,128)(2,1)}, bf16[2304,512]{1,0:T(8,128)(2,1)}, u32[]{:S(2)}, u32[]{:S(2)}) %collective-permute-start.12) | collective-permute-done | bytes 2359328 | tf_op jit(solution)/shard_map/ppermute | solution.py:23
  225.3 5.2 %collective-permute-done.8 = bf16[2304,512]{1,0:T(8,128)(2,1)} collective-permute-done((bf16[2304,512]{1,0:T(8,128)(2,1)}, bf16[2304,512]{1,0:T(8,128)(2,1)}, u32[]{:S(2)}, u32[]{:S(2)}) %collective-permute-start.8) | collective-permute-done | bytes 2359328 | tf_op jit(solution)/shard_map/ppermute | solution.py:23
  232.8 17.8 %collective-permute-done.4 = bf16[2304,640]{1,0:T(8,128)(2,1)} collective-permute-done((bf16[2304,640]{1,0:T(8,128)(2,1)}, bf16[2304,640]{1,0:T(8,128)(2,1)}, u32[]{:S(2)}, u32[]{:S(2)}) %collective-permute-start.4) | collective-permute-done | bytes 2949152 | tf_op jit(solution)/shard_map/ppermute | solution.py:23
  253.4 7.1 %collective-permute-done = bf16[2304,640]{1,0:T(8,128)(2,1)} collective-permute-done((bf16[2304,640]{1,0:T(8,128)(2,1)}, bf16[2304,640]{1,0:T(8,128)(2,1)}, u32[]{:S(2)}, u32[]{:S(2)}) %collective-permute-start) | collective-permute-done | bytes 2949152 | tf_op jit(solution)/shard_map/ppermute | solution.py:23
  263.5 3.3 collective-permute-start.14
  267.2 39.0 %collective-permute-done.14 = bf16[576,512]{1,0:T(8,128)(2,1)S(1)} collective-permute-done((bf16[576,512]{1,0:T(8,128)(2,1)S(1)}, bf16[576,512]{1,0:T(8,128)(2,1)S(1)}, u32[]{:S(2)}, u32[]{:S(2)}) %collective-permute-start.14) | collective-permute-done | bytes 589856 | tf_op jit(solution)/shard_map/ppermute | solution.py:23
  309.8 3.3 collective-permute-done.15
  313.2 9.9 %collective-permute-done.6 = bf16[576,640]{1,0:T(8,128)(2,1)S(1)} collective-permute-done((bf16[576,640]{1,0:T(8,128)(2,1)S(1)}, bf16[576,640]{1,0:T(8,128)(2,1)S(1)}, u32[]{:S(2)}, u32[]{:S(2)}) %collective-permute-start.6) | collective-permute-done | bytes 737312 | tf_op jit(solution)/shard_map/ppermute | solution.py:23
  327.0 3.8 %collective-permute-done.7 = bf16[288,640]{1,0:T(8,128)(2,1)S(1)} collective-permute-done((bf16[288,640]{1,0:T(8,128)(2,1)S(1)}, bf16[288,640]{1,0:T(8,128)(2,1)S(1)}, u32[]{:S(2)}, u32[]{:S(2)}) %collective-permute-start.7) | collective-permute-done | bytes 368672 | tf_op jit(solution)/shard_map/ppermute | solution.py:23
  (72 shorter events, 32.7 us)
Async XLA Ops:
  7.2 80.0 %all-gather.3.cloned.1.call-start = ((), (), s32[]{:S(2)}) async-start(), calls=%async_computation.4 | async-start | bytes 10616832 | tf_op jit(solution)/shard_map/all_gather | solution.py:124
  17.8 35.1 %copy-start.3 = (s32[16]{0:T(128)S(1)}, s32[16]{0:T(128)}, u32[]{:S(2)}) copy-start(s32[16]{0:T(128)} %constant.60.clone) | copy-start | bytes 196
  17.8 35.1 %copy-start.4 = (s32[16]{0:T(128)S(1)}, s32[16]{0:T(128)}, u32[]{:S(2)}) copy-start(s32[16]{0:T(128)} %constant.59.clone) | copy-start | bytes 196
  17.8 35.3 %copy-start.1 = (s32[16]{0:T(128)S(1)}, s32[16]{0:T(128)}, u32[]{:S(2)}) copy-start(s32[16]{0:T(128)} %constant.58.clone) | copy-start | bytes 196
  17.8 35.3 %copy-start.2 = (s32[16]{0:T(128)S(1)}, s32[16]{0:T(128)}, u32[]{:S(2)}) copy-start(s32[16]{0:T(128)} %constant.57.clone) | copy-start | bytes 196
  46.0 51.7 %all-to-all-start.2 = ((bf16[8,128,512]{2,1,0:T(8,128)(2,1)}), bf16[8,128,512]{2,1,0:T(8,128)(2,1)S(1)}, u32[]{:S(2)}, u32[]{:S(2)}) async-start(bf16[8,128,512]{2,1,0:T(8,128)(2,1)} %get-tuple-element.8), calls=%async_computation.2 | async-start | bytes 2097152 | tf_op jit(solution)/shard_map/all_to_all | solution.py:133
  97.7 24.3 %all-to-all-start = ((bf16[8,128,640]{2,1,0:T(8,128)(2,1)}), bf16[8,128,640]{2,1,0:T(8,128)(2,1)S(1)}, u32[]{:S(2)}, u32[]{:S(2)}) async-start(bf16[8,128,640]{2,1,0:T(8,128)(2,1)} %get-tuple-element.6), calls=%async_computation | async-start | bytes 2621440 | tf_op jit(solution)/shard_map/all_to_all | solution.py:133
  122.0 20.5 %all-to-all-start.1 = ((bf16[8,128,640]{2,1,0:T(8,128)(2,1)}), bf16[8,128,640]{2,1,0:T(8,128)(2,1)}, u32[]{:S(2)}, u32[]{:S(2)}) async-start(bf16[8,128,640]{2,1,0:T(8,128)(2,1)} %get-tuple-element.7), calls=%async_computation.1 | async-start | bytes 2621440 | tf_op jit(solution)/shard_map/all_to_all | solution.py:133
  126.8 3.7 %copy-start.5 = (f32[1024,1024]{0,1:T(8,128)S(1)}, f32[1024,1024]{0,1:T(8,128)}, u32[]{:S(2)}) copy-start(f32[1024,1024]{0,1:T(8,128)} %fusion.8) | copy-start | bytes 12582916
  160.5 3.7 %copy-start = (bf16[4608,1024]{1,0:T(8,128)(2,1)S(1)}, bf16[4608,1024]{1,0:T(8,128)(2,1)}, u32[]{:S(2)}) copy-start(bf16[4608,1024]{1,0:T(8,128)(2,1)} %shard_map.78) | copy-start | bytes 28311556
  168.5 54.0 %collective-permute-start.12 = (bf16[2304,512]{1,0:T(8,128)(2,1)}, bf16[2304,512]{1,0:T(8,128)(2,1)}, u32[]{:S(2)}, u32[]{:S(2)}) collective-permute-start(bf16[2304,512]{1,0:T(8,128)(2,1)} %shard_map.87), channel_id=1, source_target_pairs={{0,24},{8,16},{16,8},{24,0},{32,56},{40,48},{48,40},{56,32},{64,88... | collective-permute-start | bytes 7077896 | tf_op jit(solution)/shard_map/ppermute | solution.py:23
  175.9 54.5 %collective-permute-start.8 = (bf16[2304,512]{1,0:T(8,128)(2,1)}, bf16[2304,512]{1,0:T(8,128)(2,1)}, u32[]{:S(2)}, u32[]{:S(2)}) collective-permute-start(bf16[2304,512]{1,0:T(8,128)(2,1)} %shard_map.85), channel_id=1, source_target_pairs={{0,8},{8,0},{16,24},{24,16},{32,40},{40,32},{48,56},{56,48},{64,72... | collective-permute-start | bytes 7077896 | tf_op jit(solution)/shard_map/ppermute | solution.py:23
  183.7 67.0 %collective-permute-start.4 = (bf16[2304,640]{1,0:T(8,128)(2,1)}, bf16[2304,640]{1,0:T(8,128)(2,1)}, u32[]{:S(2)}, u32[]{:S(2)}) collective-permute-start(bf16[2304,640]{1,0:T(8,128)(2,1)} %shard_map.83), channel_id=1, source_target_pairs={{0,96},{8,104},{16,112},{24,120},{32,64},{40,72},{48,80},{56,88},{... | collective-permute-start | bytes 8847368 | tf_op jit(solution)/shard_map/ppermute | solution.py:23
  193.3 67.1 %collective-permute-start = (bf16[2304,640]{1,0:T(8,128)(2,1)}, bf16[2304,640]{1,0:T(8,128)(2,1)}, u32[]{:S(2)}, u32[]{:S(2)}) collective-permute-start(bf16[2304,640]{1,0:T(8,128)(2,1)} %shard_map.81), channel_id=1, source_target_pairs={{0,32},{8,40},{16,48},{24,56},{32,0},{40,8},{48,16},{56,24},{64,96... | collective-permute-start | bytes 8847368 | tf_op jit(solution)/shard_map/ppermute | solution.py:23
  224.9 38.2 %collective-permute-start.13 = (bf16[1152,512]{1,0:T(8,128)(2,1)S(1)}, bf16[1152,512]{1,0:T(8,128)(2,1)S(1)}, u32[]{:S(2)}, u32[]{:S(2)}) collective-permute-start(bf16[1152,512]{1,0:T(8,128)(2,1)S(1)} %get-tuple-element.19), channel_id=1, source_target_pairs={{0,8},{8,0},{16,24},{24,16},{32,40},{40,32},{48,56},{56,48},{64,72... | collective-permute-start | bytes 3538952 | tf_op jit(solution)/shard_map/ppermute | solution.py:23
  232.7 34.0 %collective-permute-start.9 = (bf16[1152,512]{1,0:T(8,128)(2,1)S(1)}, bf16[1152,512]{1,0:T(8,128)(2,1)S(1)}, u32[]{:S(2)}, u32[]{:S(2)}) collective-permute-start(bf16[1152,512]{1,0:T(8,128)(2,1)S(1)} %get-tuple-element.17), channel_id=1, source_target_pairs={{0,24},{8,16},{16,8},{24,0},{32,56},{40,48},{48,40},{56,32},{64,88... | collective-permute-start | bytes 3538952 | tf_op jit(solution)/shard_map/ppermute | solution.py:23
  253.2 53.2 %collective-permute-start.5 = (bf16[1152,640]{1,0:T(8,128)(2,1)S(1)}, bf16[1152,640]{1,0:T(8,128)(2,1)S(1)}, u32[]{:S(2)}, u32[]{:S(2)}) collective-permute-start(bf16[1152,640]{1,0:T(8,128)(2,1)S(1)} %get-tuple-element.15), channel_id=1, source_target_pairs={{0,32},{8,40},{16,48},{24,56},{32,0},{40,8},{48,16},{56,24},{64,96... | collective-permute-start | bytes 4423688 | tf_op jit(solution)/shard_map/ppermute | solution.py:23
  263.0 44.9 %collective-permute-start.1 = (bf16[1152,640]{1,0:T(8,128)(2,1)S(1)}, bf16[1152,640]{1,0:T(8,128)(2,1)S(1)}, u32[]{:S(2)}, u32[]{:S(2)}) collective-permute-start(bf16[1152,640]{1,0:T(8,128)(2,1)S(1)} %get-tuple-element.13), channel_id=1, source_target_pairs={{0,96},{8,104},{16,112},{24,120},{32,64},{40,72},{48,80},{56,88},{... | collective-permute-start | bytes 4423688 | tf_op jit(solution)/shard_map/ppermute | solution.py:23
  263.5 42.7 %collective-permute-start.14 = (bf16[576,512]{1,0:T(8,128)(2,1)S(1)}, bf16[576,512]{1,0:T(8,128)(2,1)S(1)}, u32[]{:S(2)}, u32[]{:S(2)}) collective-permute-start(bf16[576,512]{1,0:T(8,128)(2,1)S(1)} %get-tuple-element.27), channel_id=1, source_target_pairs={{0,96},{8,104},{16,112},{24,120},{32,64},{40,72},{48,80},{56,88},{... | collective-permute-start | bytes 1769480 | tf_op jit(solution)/shard_map/ppermute | solution.py:23
  267.1 41.9 %collective-permute-start.10 = (bf16[576,512]{1,0:T(8,128)(2,1)S(1)}, bf16[576,512]{1,0:T(8,128)(2,1)S(1)}, u32[]{:S(2)}, u32[]{:S(2)}) collective-permute-start(bf16[576,512]{1,0:T(8,128)(2,1)S(1)} %get-tuple-element.25), channel_id=1, source_target_pairs={{0,32},{8,40},{16,48},{24,56},{32,0},{40,8},{48,16},{56,24},{64,96... | collective-permute-start | bytes 1769480 | tf_op jit(solution)/shard_map/ppermute | solution.py:23
  306.3 6.8 %collective-permute-start.15 = (bf16[288,512]{1,0:T(8,128)(2,1)S(1)}, bf16[288,512]{1,0:T(8,128)(2,1)S(1)}, u32[]{:S(2)}, u32[]{:S(2)}) collective-permute-start(bf16[288,512]{1,0:T(8,128)(2,1)S(1)} %add_convert_fusion.23), channel_id=1, source_target_pairs={{0,32},{8,40},{16,48},{24,56},{32,0},{40,8},{48,16},{56,24},{64,96... | collective-permute-start | bytes 884744 | tf_op jit(solution)/shard_map/ppermute | solution.py:23
  306.8 16.4 %collective-permute-start.6 = (bf16[576,640]{1,0:T(8,128)(2,1)S(1)}, bf16[576,640]{1,0:T(8,128)(2,1)S(1)}, u32[]{:S(2)}, u32[]{:S(2)}) collective-permute-start(bf16[576,640]{1,0:T(8,128)(2,1)S(1)} %get-tuple-element.23), channel_id=1, source_target_pairs={{0,24},{8,16},{16,8},{24,0},{32,56},{40,48},{48,40},{56,32},{64,88... | collective-permute-start | bytes 2211848 | tf_op jit(solution)/shard_map/ppermute | solution.py:23
  308.3 16.2 %collective-permute-start.2 = (bf16[576,640]{1,0:T(8,128)(2,1)S(1)}, bf16[576,640]{1,0:T(8,128)(2,1)S(1)}, u32[]{:S(2)}, u32[]{:S(2)}) collective-permute-start(bf16[576,640]{1,0:T(8,128)(2,1)S(1)} %get-tuple-element.21), channel_id=1, source_target_pairs={{0,8},{8,0},{16,24},{24,16},{32,40},{40,32},{48,56},{56,48},{64,72... | collective-permute-start | bytes 2211848 | tf_op jit(solution)/shard_map/ppermute | solution.py:23
  309.1 17.8 %collective-permute-start.11 = (bf16[288,512]{1,0:T(8,128)(2,1)S(1)}, bf16[288,512]{1,0:T(8,128)(2,1)S(1)}, u32[]{:S(2)}, u32[]{:S(2)}) collective-permute-start(bf16[288,512]{1,0:T(8,128)(2,1)S(1)} %add_convert_fusion.26), channel_id=1, source_target_pairs={{0,96},{8,104},{16,112},{24,120},{32,64},{40,72},{48,80},{56,88},{... | collective-permute-start | bytes 884744 | tf_op jit(solution)/shard_map/ppermute | solution.py:23
  323.2 7.6 %collective-permute-start.7 = (bf16[288,640]{1,0:T(8,128)(2,1)S(1)}, bf16[288,640]{1,0:T(8,128)(2,1)S(1)}, u32[]{:S(2)}, u32[]{:S(2)}) collective-permute-start(bf16[288,640]{1,0:T(8,128)(2,1)S(1)} %add_convert_fusion.17), channel_id=1, source_target_pairs={{0,8},{8,0},{16,24},{24,16},{32,40},{40,32},{48,56},{56,48},{64,72... | collective-permute-start | bytes 1105928 | tf_op jit(solution)/shard_map/ppermute | solution.py:23
  324.6 8.8 %collective-permute-start.3 = (bf16[288,640]{1,0:T(8,128)(2,1)S(1)}, bf16[288,640]{1,0:T(8,128)(2,1)S(1)}, u32[]{:S(2)}, u32[]{:S(2)}) collective-permute-start(bf16[288,640]{1,0:T(8,128)(2,1)S(1)} %add_convert_fusion.20), channel_id=1, source_target_pairs={{0,24},{8,16},{16,8},{24,0},{32,56},{40,48},{48,40},{56,32},{64,88... | collective-permute-start | bytes 1105928 | tf_op jit(solution)/shard_map/ppermute | solution.py:23
Sparse Core Ops, SparseCore 0:
  11.0 76.1 all-gather.2
